TPU v7x, 128 devices: a whole 4x4x4 slice. The times are simulated.
128 devices in a mesh: row: 8 (over y, x_hi), col: 16 (over z, x_lo, core).
Axes of the slice: x: 4 (x_hi: 2, x_lo: 2; x = x_hi * 2 + x_lo), y: 4, z: 4, core: 2. Of those that a mesh axis runs over, the one named last changes fastest.
Arguments:
- teacher: bfloat16 [16384, 256], replicated, may hold values from -4 to 4
- panel_ids: int32 [2048], P('col'), may hold values from 0 to 16383
- rest_ids: int32 [8, 16, 128], P('row', 'col'), may hold values from 0 to 16383
- inverse: bfloat16 [2048, 2048], replicated, may hold values from -1 to 1, as said below
Outputs:
- trailing: float32 [16, 8, 128, 8, 16, 128], P(None, 'row', None, None, 'col')
- panel_rows: bfloat16 [8, 16, 128, 2048], P('row', 'col')
Inputs may be any that keep to these rules, and one draw needn't show every extreme that they name: `inverse`: zero above the diagonal.
All inputs are finite; a program needn't handle non-finite values.
Results may differ from a plain program's by a relative error of at most 0.0049.
Values may be sent and summed in bfloat16 or wider, within the bound.
No kernel may reach another device: no remote copies, remote signals or barrier semaphores. Data moves between devices by JAX's collectives and lax.ppermute only.
A program may use at most 128 MiB of HBM per device.

v0:
```python
import jax
import jax.numpy as jnp
from jax import lax
from jax.sharding import PartitionSpec as P


def gaussian(left_rows, right_rows, inv_scale):
    sq_left = jnp.sum(jnp.square(left_rows.astype(jnp.float32)), axis=-1)
    sq_right = jnp.sum(jnp.square(right_rows.astype(jnp.float32)), axis=-1)
    inner = lax.dot_general(
        left_rows, right_rows, (((1,), (1,)), ((), ())), preferred_element_type=jnp.float32
    )
    return jnp.exp(-inv_scale * (sq_left[:, None] + sq_right[None, :] - 2.0 * inner))


def factor(rows_emb, panel_emb, inverse, inv_scale):
    kernel = gaussian(rows_emb, panel_emb, inv_scale).astype(jnp.bfloat16)
    block_width = inverse.shape[0] // 4
    pieces = []
    for block_at in range(4):
        finish = (block_at + 1) * block_width
        pieces.append(
            lax.dot_general(
                kernel[:, :finish],
                inverse[block_at * block_width : finish, :finish],
                (((1,), (1,)), ((), ())),
                preferred_element_type=jnp.float32,
            )
        )
    return jnp.concatenate(pieces, 1).astype(jnp.bfloat16)


def shards(teacher, panel_ids, rest_ids, inverse):
    n_row = lax.axis_size("row")
    n_col = lax.axis_size("col")
    row_at = lax.axis_index("row")
    col_at = lax.axis_index("col")
    stretch_rows = rest_ids.shape[2]
    inv_scale = 2.0 / teacher.shape[1]
    gathered = lax.all_gather(rest_ids, ("row", "col"), axis=0, tiled=True)
    blocks = gathered.reshape(n_row * n_col, stretch_rows)
    panel = lax.all_gather(panel_ids, "col", axis=0, tiled=True)
    panel_emb = teacher[panel]
    own_ids = lax.dynamic_slice_in_dim(blocks, row_at * n_col + col_at, 1, 0).reshape(stretch_rows)
    col_ids = lax.dynamic_slice_in_dim(
        blocks.reshape(n_row, n_col, stretch_rows), col_at, 1, 1
    ).reshape(-1)
    row_ids = lax.dynamic_slice_in_dim(
        blocks.reshape(n_col, n_row, stretch_rows), row_at, 1, 1
    ).reshape(-1)
    own_factor = factor(teacher[own_ids], panel_emb, inverse, inv_scale)
    col_emb = teacher[col_ids]
    col_factor = lax.all_gather(own_factor, "row", axis=0, tiled=True)
    row_emb = teacher[row_ids]
    kernel = gaussian(row_emb, col_emb, inv_scale)
    local_ids = lax.dynamic_slice_in_dim(blocks, col_at * n_row + row_at, 1, 0).reshape(
        stretch_rows
    )
    local_factor = factor(teacher[local_ids], panel_emb, inverse, inv_scale)
    update = lax.dot_general(
        lax.all_gather(local_factor, "col", axis=0, tiled=True),
        col_factor,
        (((1,), (1,)), ((), ())),
        preferred_element_type=jnp.float32,
    )
    rows_local = jnp.arange(n_col * stretch_rows, dtype=jnp.int32)
    row_index = (
        rows_local // stretch_rows * n_row + row_at
    ) * stretch_rows + rows_local % stretch_rows
    cols_local = jnp.arange(n_row * stretch_rows, dtype=jnp.int32)
    col_index = (
        cols_local // stretch_rows * n_col + col_at
    ) * stretch_rows + cols_local % stretch_rows
    result = kernel - update
    trailing = jnp.where(row_index[:, None] >= col_index[None, :], result, jnp.zeros_like(result))
    return (
        trailing.reshape(n_col, 1, stretch_rows, n_row, 1, stretch_rows),
        own_factor.reshape(1, 1, stretch_rows, own_factor.shape[1]),
    )


def solution(mesh):
    return jax.shard_map(
        shards,
        mesh=mesh,
        in_specs=(P(), P("col"), P("row", "col", None), P()),
        out_specs=(P(None, "row", None, None, "col", None), P("row", "col", None, None)),
        check_vma=False,
    )
```

profile of v0, /device:TPU:1, one launch (start us, length us, event | category | flops | bytes accessed | tf_op | source)
XLA Modules:
  0.0 375.2 jit_solution(5608160516560032385)
XLA Ops:
  7.2 179.5 %all_gather.12 = s32[128,1,128]{2,1,0:T(1,128)S(1)} all-gather(s32[1,1,128]{2,1,0:T(1,128)} %param.6), channel_id=1, replica_groups=mesh['row'=8,'col'=16] {'row','col'}, dimensions={0}, use_global_device_ids=true | all-gather | bytes 66048 | tf_op jit(solution)/shard_map/all_gather | solution.py:40
  186.8 5.2 %gather_fusion.4 = bf16[128,256]{1,0:T(8,128)(2,1)S(1)} fusion(bf16[16384,256]{1,0:T(8,128)(2,1)} %param.4, s32[1024]{0:T(1024)S(1)} %get-tuple-element.8), kind=kCustom, calls=%fused_computation.4 | custom fusion | bytes 131584 | tf_op jit(solution)/shard_map/gather | solution.py:51
  192.1 16.3 %all-gather = s32[16,1,128]{2,1,0:T(1,128)S(1)} all-gather(s32[1,1,128]{2,1,0:T(1,128)} %bitcast.57), channel_id=1, replica_groups=mesh['row'=8,'col'=16] {'col'}, dimensions={0}, use_global_device_ids=true | all-gather | bytes 8704 | tf_op jit(solution)/shard_map/all_gather | solution.py:42
  208.4 11.1 %gather_fusion.3 = bf16[2048,256]{1,0:T(8,128)(2,1)S(1)} fusion(bf16[16384,256]{1,0:T(8,128)(2,1)} %param.4, s32[2048]{0:T(1024)S(1)} %fusion.49), kind=kCustom, calls=%fused_computation.3 | custom fusion | bytes 2105344 | tf_op jit(solution)/shard_map/gather | solution.py:43
  220.4 1.4 convolution_convert_fusion
  221.7 1.7 convolution_convert_fusion.2
  223.5 2.4 fusion.19
  225.9 2.1 fusion.25
  228.0 0.9 pad_maximum_fusion.1
  228.9 5.2 %gather_fusion.2 = bf16[128,256]{1,0:T(8,128)(2,1)S(1)} fusion(bf16[16384,256]{1,0:T(8,128)(2,1)} %param.4, s32[1024]{0:T(1024)S(1)} %get-tuple-element.9), kind=kCustom, calls=%fused_computation.2 | custom fusion | bytes 131584 | tf_op jit(solution)/shard_map/gather | solution.py:59
  234.2 0.5 fusion.6
  234.8 1.4 convolution_convert_fusion.1
  236.1 1.7 convolution_convert_fusion.3
  237.9 2.1 fusion.22
  239.9 2.4 fusion.16
  242.4 0.8 pad_maximum_fusion
  243.3 11.3 %gather_fusion = bf16[2048,256]{1,0:T(8,128)(2,1)S(1)} fusion(bf16[16384,256]{1,0:T(8,128)(2,1)} %param.4, s32[2048]{0:T(1024)S(1)} %broadcast_clamp_fusion), kind=kCustom, calls=%fused_computation | custom fusion | bytes 2105344 | tf_op jit(solution)/shard_map/gather | solution.py:54
  254.7 7.9 %gather_fusion.1 = bf16[1024,256]{1,0:T(8,128)(2,1)S(1)} fusion(bf16[16384,256]{1,0:T(8,128)(2,1)} %param.4, s32[1024]{0:T(1024)S(1)} %broadcast_clamp_fusion.1), kind=kCustom, calls=%fused_computation.1 | custom fusion | bytes 1052672 | tf_op jit(solution)/shard_map/gather | solution.py:52
  263.2 0.8 pad_maximum_fusion.2
  264.0 30.3 %all-gather.6.cloned.1.call-done = bf16[1024,2048]{1,0:T(8,128)(2,1)} async-done(((bf16[128,2048]{1,0:T(8,128)(2,1)}), bf16[1024,2048]{1,0:T(8,128)(2,1)}) %all-gather.6.cloned.1.call-update) | async-done | bytes 4194320 | tf_op jit(solution)/shard_map/all_gather | solution.py:53
  294.4 53.2 %all-gather.4.cloned.1.call-done = bf16[2048,2048]{1,0:T(8,128)(2,1)} async-done(((bf16[128,2048]{1,0:T(8,128)(2,1)}), bf16[2048,2048]{1,0:T(8,128)(2,1)}) %all-gather.4.cloned.1.call-update) | async-done | bytes 8388624 | tf_op jit(solution)/shard_map/all_gather | solution.py:61
  347.6 12.5 %fusion.65 = f32[2048,1024]{1,0:T(8,128)S(1)} fusion(bf16[2048,2048]{1,0:T(8,128)(2,1)} %all-gather.4.cloned.1.call-done, bf16[1024,2048]{1,0:T(8,128)(2,1)} %all-gather.6.cloned.1.call-done), kind=kOutput, calls=%fused_computation.96 | convolution fusion | flops 8589934592 | bytes 20971520 | tf_op jit(solution)/shard_map/dot_general | solution.py:60
  360.1 2.8 select_bitcast_fusion
  362.9 5.5 %copy.8 = f32[256,8,8,128]{3,2,1,0:T(8,128)} copy(f32[256,8,8,128]{3,1,2,0:T(8,128)S(1)} %select_bitcast_fusion) | data formatting | bytes 16777216
  (19 shorter events, 1.8 us)
Async XLA Ops:
  7.2 287.2 %all-gather.6.cloned.1.call-start = ((), (), s32[]{:S(2)}) async-start(), calls=%async_computation.1 | async-start | bytes 4718592 | tf_op jit(solution)/shard_map/all_gather | solution.py:53
  228.9 118.7 %all-gather.4.cloned.1.call-start = ((), (), s32[]{:S(2)}) async-start(), calls=%async_computation | async-start | bytes 8912896 | tf_op jit(solution)/shard_map/all_gather | solution.py:61
Sparse Core Ops, SparseCore 0:
  229.0 65.3 all-gather.5
  296.6 50.8 all-gather.3
where the time goes:
time: 376 us; the launch traced here: 375 us
  blocking collectives  196 us (52%)
  waiting for transfers between devices  83.6 us (22%)
  local copies, waits for them, and re-layouts  46.3 us (12%)
  matrix products  31.4 us (8%)
  between operations  14.2 us (4%)
  other arithmetic  3.77 us (1%)
    all_gather x1, blocking collectives, shards(): gathered = lax.all_gather(rest_ids, ('row', 'col'), axis=0, tiled=True)  180 us
    all_gather x1, waiting for transfers between devices, shards(): lax.all_gather(local_factor, 'col', axis=0, tiled=True)  53.2 us
    all_gather x1, waiting for transfers between devices, shards(): col_factor = lax.all_gather(own_factor, 'row', axis=0, tiled=True)  30.3 us
    all_gather x1, blocking collectives, shards(): panel = lax.all_gather(panel_ids, 'col', axis=0, tiled=True)  16.3 us
    dot_general x8, matrix products, factor(): lax.dot_general(kernel[:, :finish], inverse[block_at * block_width:finish...  15.1 us
    dot_general x1, matrix products, shards(): lax.dot_general(lax.all_gather(local_factor, 'col', axis=0, tiled=True),...  12.5 us
    gather x1, local copies, waits for them, and re-layouts, shards(): row_emb = teacher[row_ids]  11.3 us
    gather x1, local copies, waits for them, and re-layouts, shards(): panel_emb = teacher[panel]  11.1 us
  transfers between devices with their start and end apart: 2, of which 2 were waited for; matrix products, arithmetic and copies ran while one was open for 9% of the time, Pallas kernels for 0%

commit v1 on v0

--- a/solution.py
+++ b/solution.py
@@ -37,7 +37,10 @@
     col_at = lax.axis_index("col")
     stretch_rows = rest_ids.shape[2]
     inv_scale = 2.0 / teacher.shape[1]
-    gathered = lax.all_gather(rest_ids, ("row", "col"), axis=0, tiled=True)
+    size = lax.axis_size(("row", "col"))
+    parts = jnp.stack([rest_ids for _ in range(size)])
+    parts = lax.all_to_all(parts, ("row", "col"), split_axis=0, concat_axis=0)
+    gathered = jnp.concatenate(parts, axis=0)
     blocks = gathered.reshape(n_row * n_col, stretch_rows)
     panel = lax.all_gather(panel_ids, "col", axis=0, tiled=True)
     panel_emb = teacher[panel]

time: 376 us -> 217 us (0.58)
  blocking collectives: 196 us -> 20.6 us
  starting transfers between devices: 0.08 us -> 11.6 us
    all_gather x1 -> x0, blocking collectives: 180 us -> none  [shards(): gathered = lax.all_gather(rest_ids, ('row', 'col'), axis=0, tiled=True)]
    all_to_all x0 -> x1, starting transfers between devices: none -> 11.5 us  [shards(): parts = lax.all_to_all(parts, ('row', 'col'), split_axis=0, concat_axis=0)]
    all_gather x1, blocking collectives: 16.3 us -> 20.6 us  [shards(): panel = lax.all_gather(panel_ids, 'col', axis=0, tiled=True)]
  transfers between devices with their start and end apart: 2 -> 3, of which waited for: 2 -> 2; matrix products, arithmetic and copies ran while one was open for 9% -> 22% of each run, Pallas kernels for 0% -> 0%
where the time goes in v1:
time: 217 us; the launch traced here: 216 us
  waiting for transfers between devices  87 us (40%)
  local copies, waits for them, and re-layouts  47.6 us (22%)
  matrix products  31.6 us (15%)
  blocking collectives  20.6 us (9%)
  between operations  14.3 us (7%)
  starting transfers between devices  11.6 us (5%)
  other arithmetic  3.77 us (2%)
    all_gather x1, waiting for transfers between devices, shards(): lax.all_gather(local_factor, 'col', axis=0, tiled=True)  53.2 us
    all_gather x1, waiting for transfers between devices, shards(): col_factor = lax.all_gather(own_factor, 'row', axis=0, tiled=True)  33.7 us
    all_gather x1, blocking collectives, shards(): panel = lax.all_gather(panel_ids, 'col', axis=0, tiled=True)  20.6 us
    dot_general x8, matrix products, factor(): lax.dot_general(kernel[:, :finish], inverse[block_at * block_width:finish...  15.3 us
    dot_general x1, matrix products, shards(): lax.dot_general(lax.all_gather(local_factor, 'col', axis=0, tiled=True),...  12.5 us
    all_to_all x1, starting transfers between devices, shards(): parts = lax.all_to_all(parts, ('row', 'col'), split_axis=0, concat_axis=0)  11.5 us
    gather x1, local copies, waits for them, and re-layouts, shards(): row_emb = teacher[row_ids]  11.3 us
    gather x1, local copies, waits for them, and re-layouts, shards(): panel_emb = teacher[panel]  11.1 us
  transfers between devices with their start and end apart: 3, of which 2 were waited for; matrix products, arithmetic and copies ran while one was open for 22% of the time, Pallas kernels for 0%

profile of v1, /device:TPU:1, one launch (start us, length us, event | category | flops | bytes accessed | tf_op | source)
XLA Modules:
  0.0 216.4 jit_solution(9260177902450704119)
XLA Ops:
  7.2 1.3 stack.2
  8.5 11.5 %all-to-all-start = ((s32[128,1,1,128]{3,2,1,0:T(1,128)}), s32[128,1,1,128]{3,2,1,0:T(1,128)S(1)}, u32[]{:S(2)}, u32[]{:S(2)}) async-start(s32[128,1,1,128]{3,2,1,0:T(1,128)} %stack.2), calls=%async_computation | async-start | bytes 131072 | tf_op jit(solution)/shard_map/all_to_all | solution.py:42
  20.0 20.6 %all-gather = s32[16,1,128]{2,1,0:T(1,128)S(1)} all-gather(s32[1,1,128]{2,1,0:T(1,128)} %bitcast.59), channel_id=1, replica_groups=mesh['row'=8,'col'=16] {'col'}, dimensions={0}, use_global_device_ids=true | all-gather | bytes 8704 | tf_op jit(solution)/shard_map/all_gather | solution.py:45
  40.6 11.1 %gather_fusion.3 = bf16[2048,256]{1,0:T(8,128)(2,1)S(1)} fusion(bf16[16384,256]{1,0:T(8,128)(2,1)} %param.4, s32[2048]{0:T(1024)S(1)} %fusion.49), kind=kCustom, calls=%fused_computation.3 | custom fusion | bytes 2105344 | tf_op jit(solution)/shard_map/gather | solution.py:46
  52.1 5.2 %gather_fusion.4 = bf16[128,256]{1,0:T(8,128)(2,1)S(1)} fusion(bf16[16384,256]{1,0:T(8,128)(2,1)} %param.4, s32[1024]{0:T(1024)S(1)} %get-tuple-element.8), kind=kCustom, calls=%fused_computation.4 | custom fusion | bytes 131584 | tf_op jit(solution)/shard_map/gather | solution.py:54
  58.0 1.3 convolution_convert_fusion
  59.3 1.7 convolution_convert_fusion.2
  61.1 2.4 %fusion.19 = bf16[128,512]{1,0:T(8,128)(2,1)S(1)} fusion(bf16[128,2048]{1,0:T(8,128)(2,1)S(1)} %fusion.7, bf16[2048,2048]{1,0:T(8,128)(2,1)} %param.7), kind=kOutput, calls=%fused_computation.27 | convolution fusion | flops 268500992 | bytes 2752512 | tf_op jit(solution)/shard_map/dot_general | solution.py:23
  63.5 2.1 fusion.25
  65.6 0.9 pad_maximum_fusion.1
  66.5 5.2 %gather_fusion.2 = bf16[128,256]{1,0:T(8,128)(2,1)S(1)} fusion(bf16[16384,256]{1,0:T(8,128)(2,1)} %param.4, s32[1024]{0:T(1024)S(1)} %get-tuple-element.9), kind=kCustom, calls=%fused_computation.2 | custom fusion | bytes 131584 | tf_op jit(solution)/shard_map/gather | solution.py:62
  72.4 1.4 convolution_convert_fusion.1
  73.7 1.8 convolution_convert_fusion.3
  75.5 2.2 %fusion.22 = bf16[128,512]{1,0:T(8,128)(2,1)S(1)} fusion(bf16[2048,2048]{1,0:T(8,128)(2,1)} %param.7, bf16[128,2048]{1,0:T(8,128)(2,1)S(1)} %fusion.6), kind=kOutput, calls=%fused_computation.32 | convolution fusion | flops 201392128 | bytes 2097152 | tf_op jit(solution)/shard_map/dot_general | solution.py:23
  77.7 2.4 %fusion.16 = bf16[128,512]{1,0:T(8,128)(2,1)S(1)} fusion(bf16[128,2048]{1,0:T(8,128)(2,1)S(1)} %fusion.6, bf16[2048,2048]{1,0:T(8,128)(2,1)} %param.7), kind=kOutput, calls=%fused_computation.26 | convolution fusion | flops 268500992 | bytes 2752512 | tf_op jit(solution)/shard_map/dot_general | solution.py:23
  80.1 0.8 pad_maximum_fusion
  81.1 11.3 %gather_fusion = bf16[2048,256]{1,0:T(8,128)(2,1)S(1)} fusion(bf16[16384,256]{1,0:T(8,128)(2,1)} %param.4, s32[2048]{0:T(1024)S(1)} %broadcast_clamp_fusion), kind=kCustom, calls=%fused_computation | custom fusion | bytes 2105344 | tf_op jit(solution)/shard_map/gather | solution.py:57
  92.4 7.9 %gather_fusion.1 = bf16[1024,256]{1,0:T(8,128)(2,1)S(1)} fusion(bf16[16384,256]{1,0:T(8,128)(2,1)} %param.4, s32[1024]{0:T(1024)S(1)} %broadcast_clamp_fusion.1), kind=kCustom, calls=%fused_computation.1 | custom fusion | bytes 1052672 | tf_op jit(solution)/shard_map/gather | solution.py:55
  100.9 0.8 pad_maximum_fusion.2
  101.8 33.7 %all-gather.6.cloned.1.call-done = bf16[1024,2048]{1,0:T(8,128)(2,1)} async-done(((bf16[128,2048]{1,0:T(8,128)(2,1)}), bf16[1024,2048]{1,0:T(8,128)(2,1)}) %all-gather.6.cloned.1.call-update) | async-done | bytes 4194320 | tf_op jit(solution)/shard_map/all_gather | solution.py:56
  135.5 53.2 %all-gather.4.cloned.1.call-done = bf16[2048,2048]{1,0:T(8,128)(2,1)} async-done(((bf16[128,2048]{1,0:T(8,128)(2,1)}), bf16[2048,2048]{1,0:T(8,128)(2,1)}) %all-gather.4.cloned.1.call-update) | async-done | bytes 8388624 | tf_op jit(solution)/shard_map/all_gather | solution.py:64
  188.7 12.5 %fusion.65 = f32[2048,1024]{1,0:T(8,128)S(1)} fusion(bf16[2048,2048]{1,0:T(8,128)(2,1)} %all-gather.4.cloned.1.call-done, bf16[1024,2048]{1,0:T(8,128)(2,1)} %all-gather.6.cloned.1.call-done), kind=kOutput, calls=%fused_computation.96 | convolution fusion | flops 8589934592 | bytes 20971520 | tf_op jit(solution)/shard_map/dot_general | solution.py:63
  201.3 2.7 %select_bitcast_fusion = f32[256,8,8,128]{3,1,2,0:T(8,128)S(1)} fusion(f32[2048,1024]{1,0:T(8,128)S(1)} %fusion.65, bf16[2048,256]{1,0:T(8,128)(2,1)S(1)} %gather_fusion, bf16[1024,256]{1,0:T(8,128)(2,1)S(1)} %gather_fusion.1, f32[1024]{0:T(1024)S(1)} %multiply_reduce_fusion.2, f32[2048]{0:T(1024)S(1)} %multiply_reduce_fusion.1, s32[1024]{0:T(1024)S(1)} %fusion.59, ...), kind=kOutput, calls=%fused_computation.5 | convolution fusion | flops 1088421888 | bytes 18374656 | tf_op jit(solution)/shard_map/dot_general | solution.py:10
  204.0 5.5 %copy.8 = f32[256,8,8,128]{3,2,1,0:T(8,128)} copy(f32[256,8,8,128]{3,1,2,0:T(8,128)S(1)} %select_bitcast_fusion) | data formatting | bytes 16777216
  (21 shorter events, 2.3 us)
Async XLA Ops:
  8.5 43.6 %all-to-all-start = ((s32[128,1,1,128]{3,2,1,0:T(1,128)}), s32[128,1,1,128]{3,2,1,0:T(1,128)S(1)}, u32[]{:S(2)}, u32[]{:S(2)}) async-start(s32[128,1,1,128]{3,2,1,0:T(1,128)} %stack.2), calls=%async_computation | async-start | bytes 131072 | tf_op jit(solution)/shard_map/all_to_all | solution.py:42
  20.0 115.5 %all-gather.6.cloned.1.call-start = ((), (), s32[]{:S(2)}) async-start(), calls=%async_computation.2 | async-start | bytes 4718592 | tf_op jit(solution)/shard_map/all_gather | solution.py:56
  66.5 122.3 %all-gather.4.cloned.1.call-start = ((), (), s32[]{:S(2)}) async-start(), calls=%async_computation.1 | async-start | bytes 8912896 | tf_op jit(solution)/shard_map/all_gather | solution.py:64
Sparse Core Ops, SparseCore 0:
  66.6 68.8 all-gather.5
  137.8 50.8 all-gather.3
